TPU v7x, 256 devices: a whole 4x4x8 slice. The times are simulated.
256 devices in a mesh: dp: 16 (over y, x), shard: 16 (over z, core).
Axes of the slice: x: 4, y: 4, z: 8, core: 2. Of those that a mesh axis runs over, the one named last changes fastest.
Arguments:
- grad_parts: bfloat16 [16, 16, 1536, 1536], P('dp', None, 'shard'), may hold values from -48 to 48
- momentum_owned: float32 [16, 16, 96, 1536], P('shard', None, 'dp'), may hold values from -6 to 6
- owner_table: int32 [16], replicated, may hold values from 0 to 15, each once
- step_offset: int32 [1], replicated, may hold values from 0 to 15
Outputs:
- updates: bfloat16 [16, 1536, 1536], P('dp', 'shard')
- new_momentum: float32 [16, 16, 96, 1536], P('shard', None, 'dp')
Inputs may be any that keep to these rules, and one draw needn't show every extreme that they name: `owner_table`: each owner slot is named by exactly one matrix.
All inputs are finite; a program needn't handle non-finite values.
Results may differ from a plain program's by a relative error of at most 0.0089.
Values may be sent and summed in bfloat16 or wider, within the bound.
No kernel may reach another device: no remote copies, remote signals or barrier semaphores. Data moves between devices by JAX's collectives and lax.ppermute only.
A program may use at most 64 MiB of HBM per device.

v0:
```python
import jax
import jax.numpy as jnp
from jax import lax
from jax.sharding import PartitionSpec as P

D = 1536
ITERS = 2


momentum_decay = 0.95
linear_coef = 3.4445
cubic_coef = -4.775
quintic_coef = 2.0315


def body(grad_parts, momentum_owned, owner_table, step_offset):
    shard_count = lax.axis_size("shard")
    piece_rows = grad_parts.shape[2]
    owner_slot = (owner_table + step_offset[0]) % shard_count
    slot_ids = jnp.arange(shard_count, dtype=jnp.int32)
    owner_order = jnp.sum(
        jnp.where(owner_slot[None, :] == slot_ids[:, None], slot_ids[None, :], 0), axis=1
    )
    partial_value = grad_parts[0]
    summed = lax.psum_scatter(
        partial_value.astype(jnp.float32), "dp", scatter_dimension=1, tiled=True
    )
    ordered = jnp.take(summed.astype(jnp.bfloat16), owner_order, axis=0)
    grad_rows = lax.all_to_all(ordered, "shard", split_axis=0, concat_axis=0, tiled=True)
    grad_float = grad_rows.astype(jnp.float32)
    moment = momentum_decay * momentum_owned[0] + grad_float
    nesterov = grad_float + momentum_decay * moment
    total = lax.psum(jnp.sum(nesterov * nesterov), "dp")
    iterate = (nesterov / (jnp.sqrt(total) + 1e-07)).astype(jnp.bfloat16)
    sub_rows = iterate.shape[1]
    local_count = shard_count * sub_rows
    local_rows = iterate.reshape(local_count, D)
    mixed = local_rows.astype(jnp.float32)
    for sweep in range(ITERS):
        gathered = lax.all_gather(iterate, "dp", axis=1, tiled=True).reshape(D, D)
        local_rows = iterate.reshape(local_count, D)
        gram_rows = lax.dot_general(
            local_rows, gathered, (((1,), (1,)), ((), ())), preferred_element_type=jnp.float32
        ).astype(jnp.bfloat16)
        first = jnp.dot(gram_rows, gathered, preferred_element_type=jnp.float32)
        first_low = first.astype(jnp.bfloat16).reshape(shard_count, sub_rows, D)
        gram_blocks = gram_rows.reshape(local_count, shard_count, piece_rows)
        second = jnp.einsum(
            "mgp,gpl->ml",
            gram_blocks,
            lax.all_gather(first_low, "dp", axis=1, tiled=True),
            preferred_element_type=jnp.float32,
        )
        mixed = (
            linear_coef * local_rows.astype(jnp.float32)
            + cubic_coef * first
            + quintic_coef * second
        )
        if sweep + 1 < ITERS:
            iterate = mixed.astype(jnp.bfloat16).reshape(shard_count, sub_rows, D)
    squares = lax.psum(jnp.sum(mixed * mixed), "dp")
    update = (
        (mixed * lax.rsqrt(squares / (D * D) + 1e-06))
        .astype(jnp.bfloat16)
        .reshape(shard_count, sub_rows, D)
    )
    returned = lax.all_to_all(update, "shard", split_axis=0, concat_axis=0, tiled=True)
    by_matrix = jnp.take(returned, owner_slot, axis=0)
    update_blocks = lax.all_to_all(by_matrix, "dp", split_axis=0, concat_axis=1, tiled=True)
    return (update_blocks, moment[None])


def solution(mesh):
    placed = (P("dp", None, "shard", None), P("shard", None, "dp", None), P(), P())
    return jax.shard_map(
        body,
        mesh=mesh,
        in_specs=placed,
        out_specs=(P("dp", "shard", None), P("shard", None, "dp", None)),
        check_vma=False,
    )
```

profile of v0, /device:TPU:1, one launch (start us, length us, event | category | flops | bytes accessed | tf_op | source)
XLA Modules:
  0.0 515.7 jit_solution(3553493769106621101)
XLA Ops:
  7.2 8.7 %bitcast_convert_fusion = f32[16,96,1536]{2,0,1:T(8,128)} fusion(bf16[1,16,96,1536]{3,2,1,0:T(8,128)(2,1)} %param.6), kind=kLoop, calls=%fused_computation.2 | loop fusion | flops 2359296 | bytes 14155776 | tf_op jit(solution)/shard_map/convert_element_type | solution.py:26
  16.9 94.4 %reduce-scatter.2.cloned.1.call-done = f32[16,6,1536]{2,0,1:T(8,128)} async-done(((f32[16,96,1536]{2,0,1:T(8,128)}), f32[16,6,1536]{2,0,1:T(8,128)}) %reduce-scatter.2.cloned.1.call-update) | async-done | bytes 589840 | tf_op jit(solution)/shard_map/reduce_scatter | solution.py:25
  111.2 1.1 convert_element_type.41
  112.5 0.6 gather_fusion
  113.2 23.2 %all_to_all.22 = bf16[16,6,1536]{2,1,0:T(8,128)(2,1)S(1)} all-to-all(bf16[16,6,1536]{2,1,0:T(8,128)(2,1)S(1)} %broadcast_select_fusion.1), channel_id=1, replica_groups=mesh['dp'=16,'shard'=16] {'shard'}, dimensions={0} | all-to-all | bytes 589824 | tf_op jit(solution)/shard_map/all_to_all | solution.py:29
  136.4 1.1 multiply_reduce_fusion
  137.4 31.6 %psum.14 = f32[]{:T(128)} all-reduce(f32[]{:T(128)} %multiply_reduce_fusion), channel_id=1, replica_groups=mesh['dp'=16,'shard'=16] {'dp'}, use_global_device_ids=true, to_apply=%region_3.5 | all-reduce | flops 1 | bytes 8 | tf_op jit(solution)/shard_map/psum | solution.py:33
  170.2 0.8 copy.53
  171.2 57.8 %all-gather.5.cloned.1.call-done = bf16[16,96,1536]{2,0,1:T(8,128)(2,1)} async-done(((bf16[16,6,1536]{2,0,1:T(8,128)(2,1)}), bf16[16,96,1536]{2,0,1:T(8,128)(2,1)}) %all-gather.5.cloned.1.call-update) | async-done | bytes 4718608 | tf_op jit(solution)/shard_map/all_gather | solution.py:40
  228.9 4.9 copy.54
  233.9 1.5 convolution_convert_fusion.1
  235.4 0.9 fusion.7
  236.4 0.8 copy.55
  238.2 58.0 %all-gather.7.cloned.1.call-done = bf16[16,96,1536]{2,0,1:T(8,128)(2,1)} async-done(((bf16[16,6,1536]{2,0,1:T(8,128)(2,1)}), bf16[16,96,1536]{2,0,1:T(8,128)(2,1)}) %all-gather.7.cloned.1.call-update) | async-done | bytes 4718608 | tf_op jit(solution)/shard_map/all_gather | solution.py:51
  296.2 3.2 fusion.4
  299.5 0.8 copy.57
  300.6 58.7 %all-gather.9.cloned.1.call-done = bf16[16,96,1536]{2,0,1:T(8,128)(2,1)} async-done(((bf16[16,6,1536]{2,0,1:T(8,128)(2,1)}), bf16[16,96,1536]{2,0,1:T(8,128)(2,1)}) %all-gather.9.cloned.1.call-update) | async-done | bytes 4718608 | tf_op jit(solution)/shard_map/all_gather | solution.py:40
  359.3 4.9 copy.58
  364.2 1.5 convolution_convert_fusion
  365.8 0.9 fusion.8
  366.8 0.8 copy.59
  368.5 58.0 %all-gather.11.cloned.1.call-done = bf16[16,96,1536]{2,0,1:T(8,128)(2,1)} async-done(((bf16[16,6,1536]{2,0,1:T(8,128)(2,1)}), bf16[16,96,1536]{2,0,1:T(8,128)(2,1)}) %all-gather.11.cloned.1.call-update) | async-done | bytes 4718608 | tf_op jit(solution)/shard_map/all_gather | solution.py:51
  426.6 3.9 multiply_reduce_fusion.1
  430.5 31.8 %psum.15 = f32[]{:T(128)} all-reduce(f32[]{:T(128)} %get-tuple-element.21), channel_id=1, replica_groups=mesh['dp'=16,'shard'=16] {'dp'}, use_global_device_ids=true, to_apply=%region_5.7 | all-reduce | flops 1 | bytes 8 | tf_op jit(solution)/shard_map/psum | solution.py:61
  463.0 0.8 reshape.52
  463.9 14.9 %all-to-all-start.1 = ((bf16[16,6,1536]{2,1,0:T(8,128)(2,1)}), bf16[16,6,1536]{2,1,0:T(8,128)(2,1)S(1)}, u32[]{:S(2)}, u32[]{:S(2)}) async-start(bf16[16,6,1536]{2,1,0:T(8,128)(2,1)} %reshape.52), calls=%async_computation.2 | async-start | bytes 786432 | tf_op jit(solution)/shard_map/all_to_all | solution.py:67
  478.8 14.5 %all-to-all-done.1 = bf16[16,6,1536]{2,1,0:T(8,128)(2,1)S(1)} async-done(((bf16[16,6,1536]{2,1,0:T(8,128)(2,1)}), bf16[16,6,1536]{2,1,0:T(8,128)(2,1)S(1)}, u32[]{:S(2)}, u32[]{:S(2)}) %all-to-all-start.1) | async-done | bytes 294944 | tf_op jit(solution)/shard_map/all_to_all | solution.py:67
  493.9 0.9 broadcast_select_fusion
  494.8 3.6 all-to-all-start.2
  498.3 1.2 copy.61
  499.5 8.9 %all-to-all-done.2 = bf16[16,6,1536]{2,1,0:T(8,128)(2,1)S(1)} async-done(((bf16[16,6,1536]{2,1,0:T(8,128)(2,1)}), bf16[16,6,1536]{2,1,0:T(8,128)(2,1)S(1)}, u32[]{:S(2)}, u32[]{:S(2)}) %all-to-all-start.2) | async-done | bytes 294944 | tf_op jit(solution)/shard_map/all_to_all | solution.py:69
  508.4 0.8 all_to_all.18
  (34 shorter events, 4.1 us)
Async XLA Ops:
  7.2 104.1 %reduce-scatter.2.cloned.1.call-start = ((), (), s32[]{:S(2)}) async-start(), calls=%async_computation.4 | async-start | bytes 10027008 | tf_op jit(solution)/shard_map/reduce_scatter | solution.py:25
  15.9 0.8 copy-start.1
  15.9 120.5 %copy-start = (f32[1,16,6,1536]{3,1,2,0:T(8,128)S(1)}, f32[1,16,6,1536]{3,1,2,0:T(8,128)}, u32[]{:S(2)}) copy-start(f32[1,16,6,1536]{3,1,2,0:T(8,128)} %param.7) | copy-start | bytes 1769476
  15.9 213.0 %all-gather.5.cloned.1.call-start = ((), (), s32[]{:S(2)}) async-start(), calls=%async_computation.5 | async-start | bytes 5013504 | tf_op jit(solution)/shard_map/all_gather | solution.py:40
  171.0 125.2 %all-gather.7.cloned.1.call-start = ((), (), s32[]{:S(2)}) async-start(), calls=%async_computation.6 | async-start | bytes 5013504 | tf_op jit(solution)/shard_map/all_gather | solution.py:51
  237.3 122.0 %all-gather.9.cloned.1.call-start = ((), (), s32[]{:S(2)}) async-start(), calls=%async_computation.7 | async-start | bytes 5013504 | tf_op jit(solution)/shard_map/all_gather | solution.py:40
  300.4 126.2 %all-gather.11.cloned.1.call-start = ((), (), s32[]{:S(2)}) async-start(), calls=%async_computation.8 | async-start | bytes 5013504 | tf_op jit(solution)/shard_map/all_gather | solution.py:51
  463.9 29.5 %all-to-all-start.1 = ((bf16[16,6,1536]{2,1,0:T(8,128)(2,1)}), bf16[16,6,1536]{2,1,0:T(8,128)(2,1)S(1)}, u32[]{:S(2)}, u32[]{:S(2)}) async-start(bf16[16,6,1536]{2,1,0:T(8,128)(2,1)} %reshape.52), calls=%async_computation.2 | async-start | bytes 786432 | tf_op jit(solution)/shard_map/all_to_all | solution.py:67
  494.8 13.6 %all-to-all-start.2 = ((bf16[16,6,1536]{2,1,0:T(8,128)(2,1)}), bf16[16,6,1536]{2,1,0:T(8,128)(2,1)S(1)}, u32[]{:S(2)}, u32[]{:S(2)}) async-start(bf16[16,6,1536]{2,1,0:T(8,128)(2,1)} %broadcast_select_fusion), calls=%async_computation.3 | async-start | bytes 786432 | tf_op jit(solution)/shard_map/all_to_all | solution.py:69
Sparse Core Ops, SparseCore 0:
  16.1 95.1 reduce-scatter.1
  171.1 57.7 all-gather.4
  237.4 58.7 all-gather.6
  300.5 58.7 all-gather.8
  367.7 58.7 all-gather.10
where the time goes:
time: 516 us
  waiting for transfers between devices  350 us (68%)
  blocking collectives  86.6 us (17%)
  local copies, waits for them, and re-layouts  19.4 us (4%)
  starting transfers between devices  18.9 us (4%)
  between operations  16 us (3%)
  other arithmetic  12.5 us (2%)
  matrix products  12.1 us (2%)
    all_gather x2, waiting for transfers between devices, body(): gathered = lax.all_gather(iterate, 'dp', axis=1, tiled=True).reshape(D, D)  116 us
    all_gather x2, waiting for transfers between devices, body(): lax.all_gather(first_low, 'dp', axis=1, tiled=True)  116 us
    reduce_scatter x1, waiting for transfers between devices, body(): lax.psum_scatter(partial_value.astype(jnp.float32), 'dp', scatter_dimensi...  94.4 us
    psum x1, blocking collectives, body(): squares = lax.psum(jnp.sum(mixed * mixed), 'dp')  31.8 us
    psum x1, blocking collectives, body(): total = lax.psum(jnp.sum(nesterov * nesterov), 'dp')  31.6 us
    all_to_all x1, blocking collectives, body(): lax.all_to_all(ordered, 'shard', split_axis=0, concat_axis=0, tiled=True)  23.2 us
    all_to_all x1, starting transfers between devices, body(): lax.all_to_all(update, 'shard', split_axis=0, concat_axis=0, tiled=True)  14.9 us
    all_to_all x1, waiting for transfers between devices, body(): lax.all_to_all(update, 'shard', split_axis=0, concat_axis=0, tiled=True)  14.5 us
  transfers between devices with their start and end apart: 7, of which 7 were waited for; matrix products, arithmetic and copies ran while one was open for 1% of the time, Pallas kernels for 0%

commit v1 on v0

v1 whole, which is shorter than its diff:
```python
import jax
import jax.numpy as jnp
from jax import lax
from jax.experimental import pallas as pl
from jax.experimental.pallas import tpu as pltpu
from jax.sharding import PartitionSpec as P

D = 1536
ITERS = 2
CHUNKS = 2
TILE = 512

momentum_decay = 0.95
linear_coef = 3.4445
cubic_coef = -4.775
quintic_coef = 2.0315


def swap(value, axis):
    return lax.all_to_all(value, axis, split_axis=0, concat_axis=0, tiled=True)


def xor_swap(value, axis):
    count = value.shape[0]
    step = 1
    while step < count:
        pairs = [(i, i ^ step) for i in range(count)]
        halves = value.reshape((count // (2 * step), 2, step) + value.shape[1:])
        other = lax.ppermute(halves[:, 1], axis, pairs)
        value = jnp.stack([halves[:, 0], other], axis=1).reshape(value.shape)
        step *= 2
    return value


def upper_tile(t):
    i = (t >= 3).astype(jnp.int32) + (t >= 5).astype(jnp.int32)
    return i, t - 2 * i + (i * (i - 1)) // 2


def newton_schulz_kernel(shard_ref, *refs):
    parts = refs[:CHUNKS]
    out_ref, gram_ref, poly_ref, mixed_ref, diag_ref, square_ref = refs[CHUNKS : CHUNKS + 6]
    later = refs[CHUNKS + 6 :]
    wide = D // CHUNKS
    tiles = D // TILE
    contract_last = (((1,), (1,)), ((), ()))

    def block(t):
        return pl.ds(pl.multiple_of(t * TILE, TILE), TILE)

    def sweep(sources, store, measured):
        diag_ref[...] = jnp.zeros_like(diag_ref)

        def gram_tile(t, carry):
            i, j = upper_tile(t)
            total = jnp.zeros((TILE, TILE), jnp.float32)
            for source in sources:
                total = total + lax.dot_general(
                    source[block(i), :], source[block(j), :], contract_last, preferred_element_type=jnp.float32
                )
            low = total.astype(jnp.bfloat16)
            gram_ref[block(i), block(j)] = low

            @pl.when(i != j)
            def _():
                gram_ref[block(j), block(i)] = low.T

            if measured:

                @pl.when(i == j)
                def _():
                    rows = lax.broadcasted_iota(jnp.int32, (TILE, TILE), 0)
                    columns = lax.broadcasted_iota(jnp.int32, (TILE, TILE), 1)
                    diag_ref[...] += jnp.sum(jnp.where(rows == columns, total, 0.0), axis=0, keepdims=True)

            return carry

        lax.fori_loop(0, tiles * (tiles + 1) // 2, gram_tile, 0)
        if measured:
            inverse = 1.0 / (jnp.sqrt(jnp.sum(diag_ref[...])) + 1e-07)
            cubic = cubic_coef * (inverse * inverse)
            quintic = quintic_coef * (inverse * inverse) * (inverse * inverse)
        else:
            inverse, cubic, quintic = 1.0, cubic_coef, quintic_coef

        def poly_tile(t, carry):
            i, j = upper_tile(t)
            total = jnp.dot(gram_ref[block(i), :], gram_ref[:, block(j)], preferred_element_type=jnp.float32)
            low = (cubic * gram_ref[block(i), block(j)].astype(jnp.float32) + quintic * total).astype(jnp.bfloat16)
            poly_ref[block(i), block(j)] = low

            @pl.when(i != j)
            def _():
                poly_ref[block(j), block(i)] = low.T

            return carry

        lax.fori_loop(0, tiles * (tiles + 1) // 2, poly_tile, 0)

        def mix_tile(i, carry):
            for c, source in enumerate(sources):
                total = jnp.dot(poly_ref[block(i), :], source[...], preferred_element_type=jnp.float32)
                store(i, c, (linear_coef * source[block(i), :].astype(jnp.float32) + total) * inverse)
            return carry

        lax.fori_loop(0, tiles, mix_tile, 0)

    def store_later(i, c, mixed):
        later[c][block(i), :] = mixed.astype(jnp.bfloat16)

    def store_mixed(i, c, mixed):
        mixed_ref[block(i), c * wide : (c + 1) * wide] = mixed
        square_ref[...] += jnp.sum(mixed * mixed, axis=0, keepdims=True)

    square_ref[...] = jnp.zeros_like(square_ref)
    sweep(parts, store_later, True)
    sweep(later, store_mixed, False)
    scale = lax.rsqrt(jnp.sum(square_ref[...]) / (D * D) + 1e-06)
    rows = out_ref.shape[0]
    mine = pl.ds(pl.multiple_of(shard_ref[0] * rows, rows), rows)
    out_ref[...] = (mixed_ref[mine, :] * scale).astype(jnp.bfloat16)


def newton_schulz(parts, shard_index, rows):
    wide = D // CHUNKS
    return pl.pallas_call(
        newton_schulz_kernel,
        out_shape=jax.ShapeDtypeStruct((rows, D), jnp.bfloat16),
        in_specs=[pl.BlockSpec(memory_space=pltpu.SMEM)]
        + [pl.BlockSpec(memory_space=pltpu.VMEM)] * CHUNKS,
        out_specs=pl.BlockSpec(memory_space=pltpu.VMEM),
        scratch_shapes=[
            pltpu.VMEM((D, D), jnp.bfloat16),
            pltpu.VMEM((D, D), jnp.bfloat16),
            pltpu.VMEM((D, D), jnp.float32),
            pltpu.VMEM((1, TILE), jnp.float32),
            pltpu.VMEM((1, wide), jnp.float32),
        ]
        + [pltpu.VMEM((D, wide), jnp.bfloat16)] * CHUNKS,
        compiler_params=pltpu.CompilerParams(vmem_limit_bytes=44 * 1024 * 1024),
        cost_estimate=pl.CostEstimate(
            flops=2 * ITERS * 7 * D * D * D // 3, bytes_accessed=D * D * 2, transcendentals=0
        ),
        name="newton_schulz",
    )(shard_index, *parts)


def body(grad_parts, momentum_owned, owner_table, step_offset):
    shard_count = lax.axis_size("shard")
    replica, shard = lax.axis_index("dp"), lax.axis_index("shard")
    piece_rows = grad_parts.shape[2]
    sub_rows = momentum_owned.shape[2]
    owner_slot = (owner_table + step_offset[0]) % shard_count
    slot_ids = jnp.arange(shard_count, dtype=jnp.int32)
    owner_order = jnp.sum(
        jnp.where(owner_slot[None, :] == slot_ids[:, None], slot_ids[None, :], 0), axis=1
    )
    momentum = momentum_owned[0]

    by_slot = xor_swap(jnp.take(momentum.astype(jnp.bfloat16), slot_ids ^ shard, axis=0), "shard")
    by_matrix = jnp.take(by_slot, jnp.take(owner_slot, slot_ids ^ replica) ^ shard, axis=0)
    own_momentum = jnp.take(xor_swap(by_matrix, "dp"), slot_ids ^ replica, axis=0).reshape(piece_rows, D)

    wide = D // CHUNKS
    grads, gathered = [], []
    for c in range(CHUNKS):
        columns = slice(c * wide, (c + 1) * wide)
        parts = swap(grad_parts[0, :, :, columns], "dp")
        summed = lax.optimization_barrier(jnp.sum(parts.astype(jnp.float32), axis=0))
        grad = summed.astype(jnp.bfloat16)
        grad_float = grad.astype(jnp.float32)
        moment_here = momentum_decay * own_momentum[:, columns].astype(jnp.float32) + grad_float
        nesterov = (grad_float + momentum_decay * moment_here).astype(jnp.bfloat16)
        grads.append(grad)
        gathered.append(lax.all_gather(nesterov, "shard", axis=0, tiled=True))

    grad = jnp.concatenate(grads, axis=1)
    by_matrix = swap(grad.reshape(-1, sub_rows, D), "dp")
    grad_rows = swap(jnp.take(by_matrix, owner_order, axis=0), "shard")
    moment = momentum_decay * momentum + grad_rows.astype(jnp.float32)

    update = newton_schulz(gathered, shard.astype(jnp.int32)[None], piece_rows)
    return (update[None], moment[None])


def solution(mesh):
    placed = (P("dp", None, "shard", None), P("shard", None, "dp", None), P(), P())
    return jax.shard_map(
        body,
        mesh=mesh,
        in_specs=placed,
        out_specs=(P("dp", "shard", None), P("shard", None, "dp", None)),
        check_vma=False,
    )
```

time: 516 us -> 265 us (0.51)
  waiting for transfers between devices: 350 us -> 96.2 us
  blocking collectives: 86.6 us -> 32.7 us
  Pallas kernels: 0 us -> 44.2 us
  starting transfers between devices: 18.9 us -> 43.9 us
  matrix products: 12.1 us -> 0 us
    all_gather x4 -> x2, waiting for transfers between devices: 232 us -> 42.1 us  [body(): gathered.append(lax.all_gather(nesterov, 'shard', axis=0, tiled=True))]
    reduce_scatter x1 -> x0, waiting for transfers between devices: 94.4 us -> none  [body(): lax.psum_scatter(partial_value.astype(jnp.float32), 'dp', scatter_dimensi...]
    psum x2 -> x0, blocking collectives: 63.4 us -> none  [the longest x1 31.8 us: body(): squares = lax.psum(jnp.sum(mixed * mixed), 'dp')]
    ppermute x0 -> x8, waiting for transfers between devices: none -> 45.2 us  [xor_swap(): other = lax.ppermute(halves[:, 1], axis, pairs)]
    pallas_call x0 -> x1, Pallas kernels: none -> 44.2 us  [newton_schulz(): pl.pallas_call(newton_schulz_kernel, out_shape=jax.ShapeDtypeStruct((rows...]
    ppermute x0 -> x8, starting transfers between devices: none -> 21 us  [xor_swap(): other = lax.ppermute(halves[:, 1], axis, pairs)]
    all_to_all x2 -> x3, waiting for transfers between devices: 23.4 us -> 8.22 us  [swap(): return lax.all_to_all(value, axis, split_axis=0, concat_axis=0, tiled=True)]
    dot_general x6 -> x0, matrix products: 12.1 us -> none  [the longest x2 7.17 us: body(): jnp.einsum('mgp,gpl->ml', gram_blocks, lax.all_gather(first_low, 'dp', ax...]
  transfers between devices with their start and end apart: 7 -> 13, of which waited for: 7 -> 11; matrix products, arithmetic and copies ran while one was open for 1% -> 8% of each run, Pallas kernels for 0% -> 0%
where the time goes in v1:
time: 265 us
  waiting for transfers between devices  96.2 us (36%)
  Pallas kernels  44.2 us (17%)
  starting transfers between devices  43.9 us (17%)
  blocking collectives  32.7 us (12%)
  local copies, waits for them, and re-layouts  24.1 us (9%)
  between operations  15.1 us (6%)
  other arithmetic  8.31 us (3%)
    ppermute x8, waiting for transfers between devices, xor_swap(): other = lax.ppermute(halves[:, 1], axis, pairs)  45.2 us
    pallas_call x1, Pallas kernels, newton_schulz(): pl.pallas_call(newton_schulz_kernel, out_shape=jax.ShapeDtypeStruct((rows...  44.2 us
    all_gather x2, waiting for transfers between devices, body(): gathered.append(lax.all_gather(nesterov, 'shard', axis=0, tiled=True))  42.1 us
    all_to_all x1, blocking collectives, swap(): return lax.all_to_all(value, axis, split_axis=0, concat_axis=0, tiled=True)  32.7 us
    all_to_all x3, starting transfers between devices, swap(): return lax.all_to_all(value, axis, split_axis=0, concat_axis=0, tiled=True)  22.8 us
    ppermute x8, starting transfers between devices, xor_swap(): other = lax.ppermute(halves[:, 1], axis, pairs)  21 us
    all_to_all x3, waiting for transfers between devices, swap(): return lax.all_to_all(value, axis, split_axis=0, concat_axis=0, tiled=True)  8.22 us
    unnamed x16, local copies, waits for them, and re-layouts  5.9 us
  transfers between devices with their start and end apart: 13, of which 11 were waited for; matrix products, arithmetic and copies ran while one was open for 8% of the time, Pallas kernels for 0%

profile of v1, /device:TPU:1, one launch (start us, length us, event | category | flops | bytes accessed | tf_op | source)
XLA Modules:
  0.0 264.6 jit_solution(10311297444598671495)
XLA Ops:
  7.2 4.8 %slice_bitcast_fusion = (bf16[16,96,768]{2,1,0:T(8,128)(2,1)}, bf16[16,96,768]{2,1,0:T(8,128)(2,1)}) fusion(bf16[1,16,96,1536]{3,2,1,0:T(8,128)(2,1)} %param.6), kind=kLoop, calls=%fused_computation.7 | loop fusion | bytes 9437184 | tf_op jit(solution)/shard_map/squeeze | solution.py:168
  12.0 7.7 %all-to-all-start.1 = ((bf16[16,96,768]{2,1,0:T(8,128)(2,1)}), bf16[16,96,768]{2,1,0:T(8,128)(2,1)S(1)}, u32[]{:S(2)}, u32[]{:S(2)}) async-start(bf16[16,96,768]{2,1,0:T(8,128)(2,1)} %get-tuple-element.17), calls=%async_computation.1 | async-start | bytes 4718592 | tf_op jit(solution)/shard_map/all_to_all | solution.py:20
  19.8 1.1 copy.149
  20.8 1.6 gather_fusion.1
  22.6 1.0 collective-permute-start
  25.5 1.7 collective-permute-start.1
  27.9 3.1 %collective-permute-done.1 = bf16[4,2,6,1536]{3,1,2,0:T(2,128)(2,1)S(1)} collective-permute-done((bf16[4,2,6,1536]{3,1,2,0:T(2,128)(2,1)S(1)}, bf16[4,2,6,1536]{3,1,2,0:T(2,128)(2,1)S(1)}, u32[]{:S(2)}, u32[]{:S(2)}) %collective-permute-start.1) | collective-permute-done | bytes 147488 | tf_op jit(solution)/shard_map/ppermute | solution.py:29
  32.5 3.1 %collective-permute-start.2 = (bf16[2,4,6,1536]{3,1,2,0:T(4,128)(2,1)S(1)}, bf16[2,4,6,1536]{3,1,2,0:T(4,128)(2,1)S(1)}, u32[]{:S(2)}, u32[]{:S(2)}) collective-permute-start(bf16[2,4,6,1536]{3,1,2,0:T(4,128)(2,1)S(1)} %get-tuple-element.34), channel_id=1, source_target_pairs={{0,4},{1,5},{2,6},{3,7},{4,0},{5,1},{6,2},{7,3},{8,12},{9,13},{10,... | collective-permute-start | bytes 442376 | tf_op jit(solution)/shard_map/ppermute | solution.py:29
  35.6 6.5 %collective-permute-done.2 = bf16[2,4,6,1536]{3,1,2,0:T(4,128)(2,1)S(1)} collective-permute-done((bf16[2,4,6,1536]{3,1,2,0:T(4,128)(2,1)S(1)}, bf16[2,4,6,1536]{3,1,2,0:T(4,128)(2,1)S(1)}, u32[]{:S(2)}, u32[]{:S(2)}) %collective-permute-start.2) | collective-permute-done | bytes 147488 | tf_op jit(solution)/shard_map/ppermute | solution.py:29
  43.0 6.5 %collective-permute-start.3 = (bf16[1,8,6,1536]{3,1,2,0:T(8,128)(2,1)S(1)}, bf16[1,8,6,1536]{3,1,2,0:T(8,128)(2,1)S(1)}, u32[]{:S(2)}, u32[]{:S(2)}) collective-permute-start(bf16[1,8,6,1536]{3,1,2,0:T(8,128)(2,1)S(1)} %bitcast.80), channel_id=1, source_target_pairs={{0,8},{1,9},{2,10},{3,11},{4,12},{5,13},{6,14},{7,15},{8,0},{9,1},... | collective-permute-start | bytes 442376 | tf_op jit(solution)/shard_map/ppermute | solution.py:29
  49.5 3.2 %collective-permute-done.3 = bf16[1,8,6,1536]{3,1,2,0:T(8,128)(2,1)S(1)} collective-permute-done((bf16[1,8,6,1536]{3,1,2,0:T(8,128)(2,1)S(1)}, bf16[1,8,6,1536]{3,1,2,0:T(8,128)(2,1)S(1)}, u32[]{:S(2)}, u32[]{:S(2)}) %collective-permute-start.3) | collective-permute-done | bytes 147488 | tf_op jit(solution)/shard_map/ppermute | solution.py:29
  54.4 1.6 gather_fusion.2
  56.2 1.7 collective-permute-start.4
  58.0 2.4 collective-permute-done.4
  61.3 3.1 %collective-permute-start.5 = (bf16[4,2,6,1536]{3,1,2,0:T(2,128)(2,1)S(1)}, bf16[4,2,6,1536]{3,1,2,0:T(2,128)(2,1)S(1)}, u32[]{:S(2)}, u32[]{:S(2)}) collective-permute-start(bf16[4,2,6,1536]{3,1,2,0:T(2,128)(2,1)S(1)} %bitcast.86), channel_id=1, source_target_pairs={{0,32},{16,48},{32,0},{48,16},{64,96},{80,112},{96,64},{112,80},{1... | collective-permute-start | bytes 442376 | tf_op jit(solution)/shard_map/ppermute | solution.py:29
  64.3 3.1 %collective-permute-done.5 = bf16[4,2,6,1536]{3,1,2,0:T(2,128)(2,1)S(1)} collective-permute-done((bf16[4,2,6,1536]{3,1,2,0:T(2,128)(2,1)S(1)}, bf16[4,2,6,1536]{3,1,2,0:T(2,128)(2,1)S(1)}, u32[]{:S(2)}, u32[]{:S(2)}) %collective-permute-start.5) | collective-permute-done | bytes 147488 | tf_op jit(solution)/shard_map/ppermute | solution.py:29
  68.8 6.4 %all-to-all-start = ((bf16[16,96,768]{2,1,0:T(8,128)(2,1)}), bf16[16,96,768]{2,1,0:T(8,128)(2,1)}, u32[]{:S(2)}, u32[]{:S(2)}) async-start(bf16[16,96,768]{2,1,0:T(8,128)(2,1)} %get-tuple-element.18), calls=%async_computation | async-start | bytes 4718592 | tf_op jit(solution)/shard_map/all_to_all | solution.py:20
  75.4 1.4 collective-permute-start.6
  76.8 19.2 %collective-permute-done.6 = bf16[2,4,6,1536]{3,1,2,0:T(4,128)(2,1)S(1)} collective-permute-done((bf16[2,4,6,1536]{3,1,2,0:T(4,128)(2,1)S(1)}, bf16[2,4,6,1536]{3,1,2,0:T(4,128)(2,1)S(1)}, u32[]{:S(2)}, u32[]{:S(2)}) %collective-permute-start.6) | collective-permute-done | bytes 147488 | tf_op jit(solution)/shard_map/ppermute | solution.py:29
  97.0 2.5 collective-permute-start.7
  99.5 7.5 %collective-permute-done.7 = bf16[1,8,6,1536]{3,1,2,0:T(8,128)(2,1)S(1)} collective-permute-done((bf16[1,8,6,1536]{3,1,2,0:T(8,128)(2,1)S(1)}, bf16[1,8,6,1536]{3,1,2,0:T(8,128)(2,1)S(1)}, u32[]{:S(2)}, u32[]{:S(2)}) %collective-permute-start.7) | collective-permute-done | bytes 147488 | tf_op jit(solution)/shard_map/ppermute | solution.py:29
  108.0 1.3 gather_fusion.3
  109.3 1.1 broadcast_select_fusion.1
  111.6 2.0 convert_reduce_fusion.1
  116.2 8.7 %all-to-all-start.2 = ((bf16[16,6,1536]{2,1,0:T(8,128)(2,1)}), bf16[16,6,1536]{2,1,0:T(8,128)(2,1)S(1)}, u32[]{:S(2)}, u32[]{:S(2)}) async-start(bf16[16,6,1536]{2,1,0:T(8,128)(2,1)} %reshape.63), calls=%async_computation.2 | async-start | bytes 786432 | tf_op jit(solution)/shard_map/all_to_all | solution.py:20
  124.9 8.2 %all-to-all-done.2 = bf16[16,6,1536]{2,1,0:T(8,128)(2,1)S(1)} async-done(((bf16[16,6,1536]{2,1,0:T(8,128)(2,1)}), bf16[16,6,1536]{2,1,0:T(8,128)(2,1)S(1)}, u32[]{:S(2)}, u32[]{:S(2)}) %all-to-all-start.2) | async-done | bytes 294944 | tf_op jit(solution)/shard_map/all_to_all | solution.py:20
  133.8 32.7 %all_to_all.20 = bf16[16,6,1536]{2,1,0:T(8,128)(2,1)S(1)} all-to-all(bf16[16,6,1536]{2,1,0:T(8,128)(2,1)S(1)} %broadcast_select_fusion), channel_id=1, replica_groups=mesh['dp'=16,'shard'=16] {'shard'}, dimensions={0} | all-to-all | bytes 589824 | tf_op jit(solution)/shard_map/all_to_all | solution.py:20
  167.0 1.2 copy.122
  169.0 41.2 %all-gather.5.cloned.1.call-done.refs_1_ = bf16[1536,768]{1,0:T(8,128)(2,1)} async-done(((bf16[96,768]{1,0:T(8,128)(2,1)}), bf16[1536,768]{1,0:T(8,128)(2,1)}) %all-gather.5.cloned.1.call-update) | async-done | bytes 2359312 | tf_op jit(solution)/shard_map/all_gather | solution.py:175
  210.2 1.7 copy-done
  211.9 1.7 copy-done.1
  213.5 44.2 %newton_schulz.1 = bf16[96,1536]{1,0:T(8,128)(2,1)} custom-call(s32[1]{0:T(128)} %bitcast.shard_ref, bf16[1536,768]{1,0:T(8,128)(2,1)S(1)} %copy-done, bf16[1536,768]{1,0:T(8,128)(2,1)S(1)} %copy-done.1), custom_call_target="tpu_custom_call" | custom-call | flops 33822867456 | bytes 4718592 | tf_op jit(solution)/shard_map/newton_schulz/pallas_call | solution.py:126
  (79 shorter events, 16.4 us)
Async XLA Ops:
  12.0 7.8 %copy-start.2 = (f32[1,16,6,1536]{3,1,2,0:T(8,128)S(1)}, f32[1,16,6,1536]{3,1,2,0:T(8,128)}, u32[]{:S(2)}) copy-start(f32[1,16,6,1536]{3,1,2,0:T(8,128)} %param.7) | copy-start | bytes 1769476
  12.0 56.8 %all-to-all-start.1 = ((bf16[16,96,768]{2,1,0:T(8,128)(2,1)}), bf16[16,96,768]{2,1,0:T(8,128)(2,1)S(1)}, u32[]{:S(2)}, u32[]{:S(2)}) async-start(bf16[16,96,768]{2,1,0:T(8,128)(2,1)} %get-tuple-element.17), calls=%async_computation.1 | async-start | bytes 4718592 | tf_op jit(solution)/shard_map/all_to_all | solution.py:20
  19.7 4.7 %copy-start.4 = (s32[16]{0:T(128)S(1)}, s32[16]{0:T(128)}, u32[]{:S(2)}) copy-start(s32[16]{0:T(128)} %param.8) | copy-start | bytes 196
  22.6 2.0 collective-permute-start
  25.5 5.5 %collective-permute-start.1 = (bf16[4,2,6,1536]{3,1,2,0:T(2,128)(2,1)S(1)}, bf16[4,2,6,1536]{3,1,2,0:T(2,128)(2,1)S(1)}, u32[]{:S(2)}, u32[]{:S(2)}) collective-permute-start(bf16[4,2,6,1536]{3,1,2,0:T(2,128)(2,1)S(1)} %bitcast.82), channel_id=1, source_target_pairs={{0,2},{1,3},{2,0},{3,1},{4,6},{5,7},{6,4},{7,5},{8,10},{9,11},{10,... | collective-permute-start | bytes 442376 | tf_op jit(solution)/shard_map/ppermute | solution.py:29
  32.5 9.5 %collective-permute-start.2 = (bf16[2,4,6,1536]{3,1,2,0:T(4,128)(2,1)S(1)}, bf16[2,4,6,1536]{3,1,2,0:T(4,128)(2,1)S(1)}, u32[]{:S(2)}, u32[]{:S(2)}) collective-permute-start(bf16[2,4,6,1536]{3,1,2,0:T(4,128)(2,1)S(1)} %get-tuple-element.34), channel_id=1, source_target_pairs={{0,4},{1,5},{2,6},{3,7},{4,0},{5,1},{6,2},{7,3},{8,12},{9,13},{10,... | collective-permute-start | bytes 442376 | tf_op jit(solution)/shard_map/ppermute | solution.py:29
  43.0 9.7 %collective-permute-start.3 = (bf16[1,8,6,1536]{3,1,2,0:T(8,128)(2,1)S(1)}, bf16[1,8,6,1536]{3,1,2,0:T(8,128)(2,1)S(1)}, u32[]{:S(2)}, u32[]{:S(2)}) collective-permute-start(bf16[1,8,6,1536]{3,1,2,0:T(8,128)(2,1)S(1)} %bitcast.80), channel_id=1, source_target_pairs={{0,8},{1,9},{2,10},{3,11},{4,12},{5,13},{6,14},{7,15},{8,0},{9,1},... | collective-permute-start | bytes 442376 | tf_op jit(solution)/shard_map/ppermute | solution.py:29
  56.2 4.3 %collective-permute-start.4 = (bf16[8,1,6,1536]{3,0,2,1:T(8,128)(2,1)S(1)}, bf16[8,1,6,1536]{3,0,2,1:T(8,128)(2,1)S(1)}, u32[]{:S(2)}, u32[]{:S(2)}) collective-permute-start(bf16[8,1,6,1536]{3,0,2,1:T(8,128)(2,1)S(1)} %bitcast.90), channel_id=1, source_target_pairs={{0,16},{16,0},{32,48},{48,32},{64,80},{80,64},{96,112},{112,96},{1... | collective-permute-start | bytes 442376 | tf_op jit(solution)/shard_map/ppermute | solution.py:29
  61.3 6.2 %collective-permute-start.5 = (bf16[4,2,6,1536]{3,1,2,0:T(2,128)(2,1)S(1)}, bf16[4,2,6,1536]{3,1,2,0:T(2,128)(2,1)S(1)}, u32[]{:S(2)}, u32[]{:S(2)}) collective-permute-start(bf16[4,2,6,1536]{3,1,2,0:T(2,128)(2,1)S(1)} %bitcast.86), channel_id=1, source_target_pairs={{0,32},{16,48},{32,0},{48,16},{64,96},{80,112},{96,64},{112,80},{1... | collective-permute-start | bytes 442376 | tf_op jit(solution)/shard_map/ppermute | solution.py:29
  68.8 42.7 %all-to-all-start = ((bf16[16,96,768]{2,1,0:T(8,128)(2,1)}), bf16[16,96,768]{2,1,0:T(8,128)(2,1)}, u32[]{:S(2)}, u32[]{:S(2)}) async-start(bf16[16,96,768]{2,1,0:T(8,128)(2,1)} %get-tuple-element.18), calls=%async_computation | async-start | bytes 4718592 | tf_op jit(solution)/shard_map/all_to_all | solution.py:20
  75.2 93.8 %all-gather.3.cloned.1.call-start = ((), (), s32[]{:S(2)}) async-start(), calls=%async_computation.4 | async-start | bytes 2506752 | tf_op jit(solution)/shard_map/all_gather | solution.py:175
  75.4 20.6 %collective-permute-start.6 = (bf16[2,4,6,1536]{3,1,2,0:T(4,128)(2,1)S(1)}, bf16[2,4,6,1536]{3,1,2,0:T(4,128)(2,1)S(1)}, u32[]{:S(2)}, u32[]{:S(2)}) collective-permute-start(bf16[2,4,6,1536]{3,1,2,0:T(4,128)(2,1)S(1)} %get-tuple-element.28), channel_id=1, source_target_pairs={{0,64},{16,80},{32,96},{48,112},{64,0},{80,16},{96,32},{112,48},{1... | collective-permute-start | bytes 442376 | tf_op jit(solution)/shard_map/ppermute | solution.py:29
  97.0 10.0 %collective-permute-start.7 = (bf16[1,8,6,1536]{3,1,2,0:T(8,128)(2,1)S(1)}, bf16[1,8,6,1536]{3,1,2,0:T(8,128)(2,1)S(1)}, u32[]{:S(2)}, u32[]{:S(2)}) collective-permute-start(bf16[1,8,6,1536]{3,1,2,0:T(8,128)(2,1)S(1)} %bitcast.84), channel_id=1, source_target_pairs={{0,128},{16,144},{32,160},{48,176},{64,192},{80,208},{96,224},{112... | collective-permute-start | bytes 442376 | tf_op jit(solution)/shard_map/ppermute | solution.py:29
  111.2 2.3 copy-start.3
  114.4 95.8 %all-gather.5.cloned.1.call-start = ((), (), s32[]{:S(2)}) async-start(), calls=%async_computation.5 | async-start | bytes 2506752 | tf_op jit(solution)/shard_map/all_gather | solution.py:175
  116.2 17.0 %all-to-all-start.2 = ((bf16[16,6,1536]{2,1,0:T(8,128)(2,1)}), bf16[16,6,1536]{2,1,0:T(8,128)(2,1)S(1)}, u32[]{:S(2)}, u32[]{:S(2)}) async-start(bf16[16,6,1536]{2,1,0:T(8,128)(2,1)} %reshape.63), calls=%async_computation.2 | async-start | bytes 786432 | tf_op jit(solution)/shard_map/all_to_all | solution.py:20
  210.2 1.7 copy-start
  211.9 1.7 copy-start.1
Sparse Core Ops, SparseCore 0:
  114.6 54.4 all-gather.2
  171.4 38.7 all-gather.4

commit v2 on v1

v2 whole, which is shorter than its diff:
```python
import jax
import jax.numpy as jnp
from jax import lax
from jax.experimental import pallas as pl
from jax.experimental.pallas import tpu as pltpu
from jax.sharding import PartitionSpec as P

D = 1536
ITERS = 2
TILE = 512

momentum_decay = 0.95
linear_coef = 3.4445
cubic_coef = -4.775
quintic_coef = 2.0315


def swap(value, axis):
    return lax.all_to_all(value, axis, split_axis=0, concat_axis=0, tiled=True)


def xor_swap(value, axis):
    count = value.shape[0]
    step = 1
    while step < count:
        pairs = [(i, i ^ step) for i in range(count)]
        halves = value.reshape((count // (2 * step), 2, step) + value.shape[1:])
        other = lax.ppermute(halves[:, 1], axis, pairs)
        value = jnp.stack([halves[:, 0], other], axis=1).reshape(value.shape)
        step *= 2
    return value


def newton_schulz_kernel(place_ref, whole_ref, out_ref, first_ref, later_ref, gram_ref, poly_ref, mixed_ref, diag_ref, square_ref, sems):
    half = D // 2
    tiles = D // TILE
    contract_last = (((1,), (1,)), ((), ()))
    copies = [
        pltpu.make_async_copy(
            whole_ref.at[pl.ds(h * half, half), :], first_ref.at[pl.ds(h * half, half), :], sems.at[h]
        )
        for h in range(2)
    ]
    for copy in copies:
        copy.start()
    diag_ref[...] = jnp.zeros_like(diag_ref)
    square_ref[...] = jnp.zeros_like(square_ref)
    for copy in copies:
        copy.wait()

    def span(start, size):
        return pl.ds(pl.multiple_of(start, 256), size)

    def symmetric(product, finish, target):
        def step(t, carry):
            i = (t >= 2).astype(jnp.int32) * TILE
            j = (1 + (t >= 1).astype(jnp.int32)) * TILE
            k = t * TILE
            small = TILE // 2
            for row, column, height, diagonal in (
                (i, j, TILE, False),
                (i, j + small, TILE, False),
                (k, k, TILE, True),
                (k + small, k + small, small, True),
            ):
                low = finish(row, column, height, diagonal, product(row, column, height))
                target[span(row, height), span(column, small)] = low
                if not diagonal:
                    target[span(column, small), span(row, height)] = low.T
                elif height == TILE:
                    target[span(column, small), span(row + small, small)] = low[small:, :].T
            return carry

        lax.fori_loop(0, tiles, step, 0)

    def sweep(source, store, measured):
        def gram_product(row, column, height):
            return lax.dot_general(
                source[span(row, height), :],
                source[span(column, TILE // 2), :],
                contract_last,
                preferred_element_type=jnp.float32,
            )

        def gram_finish(row, column, height, diagonal, total):
            if measured and diagonal:
                rows = lax.broadcasted_iota(jnp.int32, total.shape, 0)
                columns = lax.broadcasted_iota(jnp.int32, total.shape, 1)
                diag_ref[...] += jnp.sum(jnp.where(rows == columns, total, 0.0), axis=0, keepdims=True)
            return total.astype(jnp.bfloat16)

        symmetric(gram_product, gram_finish, gram_ref)
        if measured:
            inverse = 1.0 / (jnp.sqrt(jnp.sum(diag_ref[...])) + 1e-07)
            cubic = cubic_coef * (inverse * inverse)
            quintic = quintic_coef * (inverse * inverse) * (inverse * inverse)
        else:
            inverse, cubic, quintic = 1.0, cubic_coef, quintic_coef

        def poly_product(row, column, height):
            return jnp.dot(
                gram_ref[span(row, height), :], gram_ref[:, span(column, TILE // 2)], preferred_element_type=jnp.float32
            )

        def poly_finish(row, column, height, diagonal, total):
            gram = gram_ref[span(row, height), span(column, TILE // 2)].astype(jnp.float32)
            return (cubic * gram + quintic * total).astype(jnp.bfloat16)

        symmetric(poly_product, poly_finish, poly_ref)

        def mix_tile(t, carry):
            rows = span(t * TILE, TILE)
            for c in range(0, D, TILE // 2):
                columns = slice(c, c + TILE // 2)
                total = jnp.dot(poly_ref[rows, :], source[:, columns], preferred_element_type=jnp.float32)
                store(rows, columns, (linear_coef * source[rows, columns].astype(jnp.float32) + total) * inverse)
            return carry

        lax.fori_loop(0, tiles, mix_tile, 0)

    def store_later(rows, columns, mixed):
        later_ref[rows, columns] = mixed.astype(jnp.bfloat16)

    def store_mixed(rows, columns, mixed):
        mixed_ref[rows, columns] = mixed
        square_ref[:, columns] += jnp.sum(mixed * mixed, axis=0, keepdims=True)

    sweep(first_ref, store_later, True)
    sweep(later_ref, store_mixed, False)
    scale = lax.rsqrt(jnp.sum(square_ref[...]) / (D * D) + 1e-06)
    rows = out_ref.shape[0]
    mine = pl.ds(pl.multiple_of(place_ref[0] * rows, rows), rows)
    out_ref[...] = (mixed_ref[mine, :] * scale).astype(jnp.bfloat16)


def newton_schulz(whole, place, rows):
    return pl.pallas_call(
        newton_schulz_kernel,
        out_shape=jax.ShapeDtypeStruct((rows, D), jnp.bfloat16),
        in_specs=[pl.BlockSpec(memory_space=pltpu.SMEM)] + [pl.BlockSpec(memory_space=pl.ANY)],
        out_specs=pl.BlockSpec(memory_space=pltpu.VMEM),
        scratch_shapes=[
            pltpu.VMEM((D, D), jnp.bfloat16),
            pltpu.VMEM((D, D), jnp.bfloat16),
            pltpu.VMEM((D, D), jnp.bfloat16),
            pltpu.VMEM((D, D), jnp.bfloat16),
            pltpu.VMEM((D, D), jnp.float32),
            pltpu.VMEM((1, TILE // 2), jnp.float32),
            pltpu.VMEM((1, D), jnp.float32),
            pltpu.SemaphoreType.DMA((2,)),
        ],
        compiler_params=pltpu.CompilerParams(vmem_limit_bytes=48 * 1024 * 1024),
        cost_estimate=pl.CostEstimate(
            flops=2 * ITERS * 7 * D * D * D // 3, bytes_accessed=D * D * 2, transcendentals=0
        ),
        name="newton_schulz",
    )(place, whole)


def body(grad_parts, momentum_owned, owner_table, step_offset):
    replica, shard = lax.axis_index("dp"), lax.axis_index("shard")
    mats, piece_rows = grad_parts.shape[1], grad_parts.shape[2]
    sub_rows = momentum_owned.shape[2]
    owner_slot = (owner_table + step_offset[0]) % mats
    slot_ids = jnp.arange(mats, dtype=jnp.int32)
    owner_order = jnp.sum(
        jnp.where(owner_slot[None, :] == slot_ids[:, None], slot_ids[None, :], 0), axis=1
    )
    momentum = momentum_owned[0]

    parts = swap(grad_parts[0], "dp")

    by_slot = xor_swap(jnp.take(momentum.astype(jnp.bfloat16), slot_ids ^ shard, axis=0), "shard")
    by_matrix = jnp.take(by_slot, jnp.take(owner_slot, slot_ids ^ replica) ^ shard, axis=0)
    own_momentum = jnp.take(xor_swap(by_matrix, "dp"), slot_ids ^ replica, axis=0).reshape(piece_rows, D)

    summed = lax.optimization_barrier(jnp.sum(parts.astype(jnp.float32), axis=0))
    grad = summed.astype(jnp.bfloat16)
    grad_float = grad.astype(jnp.float32)
    moment_here = momentum_decay * own_momentum.astype(jnp.float32) + grad_float
    nesterov = (grad_float + momentum_decay * moment_here).astype(jnp.bfloat16)
    whole = lax.all_gather(nesterov, "shard", axis=0, tiled=True)

    grad_blocks = swap(grad.reshape(mats, sub_rows, D), "dp")
    grad_rows = swap(jnp.take(grad_blocks, owner_order, axis=0), "shard")
    moment = momentum_decay * momentum + grad_rows.astype(jnp.float32)

    update = newton_schulz(whole, shard.astype(jnp.int32)[None], piece_rows)
    return (update[None], moment[None])


def solution(mesh):
    placed = (P("dp", None, "shard", None), P("shard", None, "dp", None), P(), P())
    return jax.shard_map(
        body,
        mesh=mesh,
        in_specs=placed,
        out_specs=(P("dp", "shard", None), P("shard", None, "dp", None)),
        check_vma=False,
    )
```

time: 265 us -> 215 us (0.81)
  waiting for transfers between devices: 96.2 us -> 77.9 us
  starting transfers between devices: 43.9 us -> 29.5 us
  local copies, waits for them, and re-layouts: 24.1 us -> 13.3 us
  Pallas kernels: 44.2 us -> 38.2 us
    all_gather x2 -> x1, waiting for transfers between devices: 42.1 us -> 7.67 us  [body(): whole = lax.all_gather(nesterov, 'shard', axis=0, tiled=True)]
    ppermute x8, waiting for transfers between devices: 45.2 us -> 62 us  [xor_swap(): other = lax.ppermute(halves[:, 1], axis, pairs)]
    all_to_all x3 -> x2, starting transfers between devices: 22.8 us -> 12.3 us  [swap(): return lax.all_to_all(value, axis, split_axis=0, concat_axis=0, tiled=True)]
    pallas_call x1, Pallas kernels: 44.2 us -> 38.2 us  [newton_schulz(): pl.pallas_call(newton_schulz_kernel, out_shape=jax.ShapeDtypeStruct((rows...]
    squeeze x1 -> x0, local copies, waits for them, and re-layouts: 4.82 us -> none  [body(): parts = swap(grad_parts[0, :, :, columns], 'dp')]
    ppermute x8, starting transfers between devices: 21 us -> 17.1 us  [xor_swap(): other = lax.ppermute(halves[:, 1], axis, pairs)]
    unnamed x16 -> x12, local copies, waits for them, and re-layouts: 5.9 us -> 4.16 us
    all_to_all x3 -> x2, waiting for transfers between devices: 8.22 us -> 8.22 us  [swap(): return lax.all_to_all(value, axis, split_axis=0, concat_axis=0, tiled=True)]
  transfers between devices with their start and end apart: 13 -> 11, of which waited for: 11 -> 10; matrix products, arithmetic and copies ran while one was open for 8% -> 7% of each run, Pallas kernels for 0% -> 0%
where the time goes in v2:
time: 215 us
  waiting for transfers between devices  77.9 us (36%)
  Pallas kernels  38.2 us (18%)
  blocking collectives  33 us (15%)
  starting transfers between devices  29.5 us (14%)
  between operations  15.1 us (7%)
  local copies, waits for them, and re-layouts  13.3 us (6%)
  other arithmetic  8 us (4%)
    ppermute x8, waiting for transfers between devices, xor_swap(): other = lax.ppermute(halves[:, 1], axis, pairs)  62 us
    pallas_call x1, Pallas kernels, newton_schulz(): pl.pallas_call(newton_schulz_kernel, out_shape=jax.ShapeDtypeStruct((rows...  38.2 us
    all_to_all x1, blocking collectives, swap(): return lax.all_to_all(value, axis, split_axis=0, concat_axis=0, tiled=True)  33 us
    ppermute x8, starting transfers between devices, xor_swap(): other = lax.ppermute(halves[:, 1], axis, pairs)  17.1 us
    all_to_all x2, starting transfers between devices, swap(): return lax.all_to_all(value, axis, split_axis=0, concat_axis=0, tiled=True)  12.3 us
    all_to_all x2, waiting for transfers between devices, swap(): return lax.all_to_all(value, axis, split_axis=0, concat_axis=0, tiled=True)  8.22 us
    all_gather x1, waiting for transfers between devices, body(): whole = lax.all_gather(nesterov, 'shard', axis=0, tiled=True)  7.67 us
  transfers between devices with their start and end apart: 11, of which 10 were waited for; matrix products, arithmetic and copies ran while one was open for 7% of the time, Pallas kernels for 0%

profile of v2, /device:TPU:1, one launch (start us, length us, event | category | flops | bytes accessed | tf_op | source)
XLA Modules:
  0.0 215.0 jit_solution(7863458750219555290)
XLA Ops:
  7.2 7.8 %all-to-all-start = ((bf16[16,96,1536]{2,1,0:T(8,128)(2,1)}), bf16[16,96,1536]{2,1,0:T(8,128)(2,1)}, u32[]{:S(2)}, u32[]{:S(2)}) async-start(bf16[16,96,1536]{2,1,0:T(8,128)(2,1)} %bitcast.68), calls=%async_computation | async-start | bytes 9437184 | tf_op jit(solution)/shard_map/all_to_all | solution.py:19
  15.4 0.6 gather_fusion.1
  16.2 1.0 collective-permute-start
  19.1 1.7 collective-permute-start.1
  20.8 0.7 gather_fusion
  21.5 3.2 %collective-permute-done.1 = bf16[4,2,6,1536]{3,1,2,0:T(2,128)(2,1)S(1)} collective-permute-done((bf16[4,2,6,1536]{3,1,2,0:T(2,128)(2,1)S(1)}, bf16[4,2,6,1536]{3,1,2,0:T(2,128)(2,1)S(1)}, u32[]{:S(2)}, u32[]{:S(2)}) %collective-permute-start.1) | collective-permute-done | bytes 147488 | tf_op jit(solution)/shard_map/ppermute | solution.py:28
  24.9 0.7 pad_maximum_fusion
  26.2 3.1 %collective-permute-start.2 = (bf16[2,4,6,1536]{3,1,2,0:T(4,128)(2,1)S(1)}, bf16[2,4,6,1536]{3,1,2,0:T(4,128)(2,1)S(1)}, u32[]{:S(2)}, u32[]{:S(2)}) collective-permute-start(bf16[2,4,6,1536]{3,1,2,0:T(4,128)(2,1)S(1)} %get-tuple-element.30), channel_id=1, source_target_pairs={{0,4},{1,5},{2,6},{3,7},{4,0},{5,1},{6,2},{7,3},{8,12},{9,13},{10,... | collective-permute-start | bytes 442376 | tf_op jit(solution)/shard_map/ppermute | solution.py:28
  29.3 6.6 %collective-permute-done.2 = bf16[2,4,6,1536]{3,1,2,0:T(4,128)(2,1)S(1)} collective-permute-done((bf16[2,4,6,1536]{3,1,2,0:T(4,128)(2,1)S(1)}, bf16[2,4,6,1536]{3,1,2,0:T(4,128)(2,1)S(1)}, u32[]{:S(2)}, u32[]{:S(2)}) %collective-permute-start.2) | collective-permute-done | bytes 147488 | tf_op jit(solution)/shard_map/ppermute | solution.py:28
  36.8 6.4 %collective-permute-start.3 = (bf16[1,8,6,1536]{3,1,2,0:T(8,128)(2,1)S(1)}, bf16[1,8,6,1536]{3,1,2,0:T(8,128)(2,1)S(1)}, u32[]{:S(2)}, u32[]{:S(2)}) collective-permute-start(bf16[1,8,6,1536]{3,1,2,0:T(8,128)(2,1)S(1)} %bitcast.78), channel_id=1, source_target_pairs={{0,8},{1,9},{2,10},{3,11},{4,12},{5,13},{6,14},{7,15},{8,0},{9,1},... | collective-permute-start | bytes 442376 | tf_op jit(solution)/shard_map/ppermute | solution.py:28
  43.3 3.3 %collective-permute-done.3 = bf16[1,8,6,1536]{3,1,2,0:T(8,128)(2,1)S(1)} collective-permute-done((bf16[1,8,6,1536]{3,1,2,0:T(8,128)(2,1)S(1)}, bf16[1,8,6,1536]{3,1,2,0:T(8,128)(2,1)S(1)}, u32[]{:S(2)}, u32[]{:S(2)}) %collective-permute-start.3) | collective-permute-done | bytes 147488 | tf_op jit(solution)/shard_map/ppermute | solution.py:28
  46.8 0.7 pad_maximum_fusion.2
  47.6 0.6 gather_fusion.2
  48.3 1.7 collective-permute-start.4
  50.1 36.4 %collective-permute-done.4 = bf16[8,1,6,1536]{3,0,2,1:T(8,128)(2,1)S(1)} collective-permute-done((bf16[8,1,6,1536]{3,0,2,1:T(8,128)(2,1)S(1)}, bf16[8,1,6,1536]{3,0,2,1:T(8,128)(2,1)S(1)}, u32[]{:S(2)}, u32[]{:S(2)}) %collective-permute-start.4) | collective-permute-done | bytes 147488 | tf_op jit(solution)/shard_map/ppermute | solution.py:28
  87.5 5.5 %collective-permute-done.5 = bf16[4,2,6,1536]{3,1,2,0:T(2,128)(2,1)S(1)} collective-permute-done((bf16[4,2,6,1536]{3,1,2,0:T(2,128)(2,1)S(1)}, bf16[4,2,6,1536]{3,1,2,0:T(2,128)(2,1)S(1)}, u32[]{:S(2)}, u32[]{:S(2)}) %collective-permute-start.5) | collective-permute-done | bytes 147488 | tf_op jit(solution)/shard_map/ppermute | solution.py:28
  93.2 0.7 pad_maximum_fusion.3
  94.8 3.9 %collective-permute-done.6 = bf16[2,4,6,1536]{3,1,2,0:T(4,128)(2,1)S(1)} collective-permute-done((bf16[2,4,6,1536]{3,1,2,0:T(4,128)(2,1)S(1)}, bf16[2,4,6,1536]{3,1,2,0:T(4,128)(2,1)S(1)}, u32[]{:S(2)}, u32[]{:S(2)}) %collective-permute-start.6) | collective-permute-done | bytes 147488 | tf_op jit(solution)/shard_map/ppermute | solution.py:28
  99.7 2.7 %collective-permute-start.7 = (bf16[1,8,6,1536]{3,1,2,0:T(8,128)(2,1)S(1)}, bf16[1,8,6,1536]{3,1,2,0:T(8,128)(2,1)S(1)}, u32[]{:S(2)}, u32[]{:S(2)}) collective-permute-start(bf16[1,8,6,1536]{3,1,2,0:T(8,128)(2,1)S(1)} %bitcast.82), channel_id=1, source_target_pairs={{0,128},{16,144},{32,160},{48,176},{64,192},{80,208},{96,224},{112... | collective-permute-start | bytes 442376 | tf_op jit(solution)/shard_map/ppermute | solution.py:28
  102.4 2.9 %collective-permute-done.7 = bf16[1,8,6,1536]{3,1,2,0:T(8,128)(2,1)S(1)} collective-permute-done((bf16[1,8,6,1536]{3,1,2,0:T(8,128)(2,1)S(1)}, bf16[1,8,6,1536]{3,1,2,0:T(8,128)(2,1)S(1)}, u32[]{:S(2)}, u32[]{:S(2)}) %collective-permute-start.7) | collective-permute-done | bytes 147488 | tf_op jit(solution)/shard_map/ppermute | solution.py:28
  105.5 0.7 pad_maximum_fusion.5
  106.3 0.6 gather_fusion.3
  107.1 3.0 %convert_reduce_fusion = bf16[96,1536]{1,0:T(8,128)(2,1)S(1)} fusion(bf16[16,96,1536]{2,1,0:T(8,128)(2,1)} %all-to-all-done), kind=kLoop, calls=%fused_computation.5 | loop fusion | flops 4571136 | bytes 5013504 | tf_op jit(solution)/shard_map/reduce_sum | solution.py:177
  110.1 0.8 fusion.4
  111.1 0.8 reshape.63
  111.9 4.5 %all-to-all-start.1 = ((bf16[16,6,1536]{2,1,0:T(8,128)(2,1)}), bf16[16,6,1536]{2,1,0:T(8,128)(2,1)S(1)}, u32[]{:S(2)}, u32[]{:S(2)}) async-start(bf16[16,6,1536]{2,1,0:T(8,128)(2,1)} %reshape.63), calls=%async_computation.1 | async-start | bytes 786432 | tf_op jit(solution)/shard_map/all_to_all | solution.py:19
  116.5 8.2 %all-to-all-done.1 = bf16[16,6,1536]{2,1,0:T(8,128)(2,1)S(1)} async-done(((bf16[16,6,1536]{2,1,0:T(8,128)(2,1)}), bf16[16,6,1536]{2,1,0:T(8,128)(2,1)S(1)}, u32[]{:S(2)}, u32[]{:S(2)}) %all-to-all-start.1) | async-done | bytes 294944 | tf_op jit(solution)/shard_map/all_to_all | solution.py:19
  125.4 33.0 %all_to_all.15 = bf16[16,6,1536]{2,1,0:T(8,128)(2,1)S(1)} all-to-all(bf16[16,6,1536]{2,1,0:T(8,128)(2,1)S(1)} %broadcast_select_fusion), channel_id=1, replica_groups=mesh['dp'=16,'shard'=16] {'shard'}, dimensions={0} | all-to-all | bytes 589824 | tf_op jit(solution)/shard_map/all_to_all | solution.py:19
  158.8 1.2 copy.122
  160.0 7.7 %all-gather.2.cloned.1.call-done.whole_ref = bf16[1536,1536]{1,0:T(8,128)(2,1)} async-done(((bf16[96,1536]{1,0:T(8,128)(2,1)}), bf16[1536,1536]{1,0:T(8,128)(2,1)}) %all-gather.2.cloned.1.call-update) | async-done | bytes 4718608 | tf_op jit(solution)/shard_map/all_gather | solution.py:182
  167.7 2.3 %copy-done = bf16[1536,1536]{1,0:T(8,128)(2,1)S(1)} copy-done((bf16[1536,1536]{1,0:T(8,128)(2,1)S(1)}, bf16[1536,1536]{1,0:T(8,128)(2,1)}, u32[]{:S(2)}) %copy-start) | copy-done | bytes 4718616
  170.0 38.2 %newton_schulz.1 = bf16[96,1536]{1,0:T(8,128)(2,1)} custom-call(s32[1]{0:T(128)} %bitcast.place_ref, bf16[1536,1536]{1,0:T(8,128)(2,1)S(1)} %copy-done), custom_call_target="tpu_custom_call" | custom-call | flops 33822867456 | bytes 4718592 | tf_op jit(solution)/shard_map/newton_schulz/pallas_call | solution.py:137
  (67 shorter events, 8.8 us)
Async XLA Ops:
  7.2 7.9 %copy-start.1 = (f32[1,16,6,1536]{3,1,2,0:T(8,128)S(1)}, f32[1,16,6,1536]{3,1,2,0:T(8,128)}, u32[]{:S(2)}) copy-start(f32[1,16,6,1536]{3,1,2,0:T(8,128)} %param.7) | copy-start | bytes 1769476
  7.2 10.8 %copy-start.2 = (s32[16]{0:T(128)S(1)}, s32[16]{0:T(128)}, u32[]{:S(2)}) copy-start(s32[16]{0:T(128)} %param.8) | copy-start | bytes 196
  7.2 99.9 %all-to-all-start = ((bf16[16,96,1536]{2,1,0:T(8,128)(2,1)}), bf16[16,96,1536]{2,1,0:T(8,128)(2,1)}, u32[]{:S(2)}, u32[]{:S(2)}) async-start(bf16[16,96,1536]{2,1,0:T(8,128)(2,1)} %bitcast.68), calls=%async_computation | async-start | bytes 9437184 | tf_op jit(solution)/shard_map/all_to_all | solution.py:19
  15.0 152.7 %all-gather.2.cloned.1.call-start = ((), (), s32[]{:S(2)}) async-start(), calls=%async_computation.3 | async-start | bytes 5013504 | tf_op jit(solution)/shard_map/all_gather | solution.py:182
  16.2 2.0 collective-permute-start
  19.1 5.6 %collective-permute-start.1 = (bf16[4,2,6,1536]{3,1,2,0:T(2,128)(2,1)S(1)}, bf16[4,2,6,1536]{3,1,2,0:T(2,128)(2,1)S(1)}, u32[]{:S(2)}, u32[]{:S(2)}) collective-permute-start(bf16[4,2,6,1536]{3,1,2,0:T(2,128)(2,1)S(1)} %bitcast.80), channel_id=1, source_target_pairs={{0,2},{1,3},{2,0},{3,1},{4,6},{5,7},{6,4},{7,5},{8,10},{9,11},{10,... | collective-permute-start | bytes 442376 | tf_op jit(solution)/shard_map/ppermute | solution.py:28
  26.2 9.7 %collective-permute-start.2 = (bf16[2,4,6,1536]{3,1,2,0:T(4,128)(2,1)S(1)}, bf16[2,4,6,1536]{3,1,2,0:T(4,128)(2,1)S(1)}, u32[]{:S(2)}, u32[]{:S(2)}) collective-permute-start(bf16[2,4,6,1536]{3,1,2,0:T(4,128)(2,1)S(1)} %get-tuple-element.30), channel_id=1, source_target_pairs={{0,4},{1,5},{2,6},{3,7},{4,0},{5,1},{6,2},{7,3},{8,12},{9,13},{10,... | collective-permute-start | bytes 442376 | tf_op jit(solution)/shard_map/ppermute | solution.py:28
  36.8 9.7 %collective-permute-start.3 = (bf16[1,8,6,1536]{3,1,2,0:T(8,128)(2,1)S(1)}, bf16[1,8,6,1536]{3,1,2,0:T(8,128)(2,1)S(1)}, u32[]{:S(2)}, u32[]{:S(2)}) collective-permute-start(bf16[1,8,6,1536]{3,1,2,0:T(8,128)(2,1)S(1)} %bitcast.78), channel_id=1, source_target_pairs={{0,8},{1,9},{2,10},{3,11},{4,12},{5,13},{6,14},{7,15},{8,0},{9,1},... | collective-permute-start | bytes 442376 | tf_op jit(solution)/shard_map/ppermute | solution.py:28
  48.3 38.2 %collective-permute-start.4 = (bf16[8,1,6,1536]{3,0,2,1:T(8,128)(2,1)S(1)}, bf16[8,1,6,1536]{3,0,2,1:T(8,128)(2,1)S(1)}, u32[]{:S(2)}, u32[]{:S(2)}) collective-permute-start(bf16[8,1,6,1536]{3,0,2,1:T(8,128)(2,1)S(1)} %bitcast.88), channel_id=1, source_target_pairs={{0,16},{16,0},{32,48},{48,32},{64,80},{80,64},{96,112},{112,96},{1... | collective-permute-start | bytes 442376 | tf_op jit(solution)/shard_map/ppermute | solution.py:28
  87.4 5.6 %collective-permute-start.5 = (bf16[4,2,6,1536]{3,1,2,0:T(2,128)(2,1)S(1)}, bf16[4,2,6,1536]{3,1,2,0:T(2,128)(2,1)S(1)}, u32[]{:S(2)}, u32[]{:S(2)}) collective-permute-start(bf16[4,2,6,1536]{3,1,2,0:T(2,128)(2,1)S(1)} %bitcast.84), channel_id=1, source_target_pairs={{0,32},{16,48},{32,0},{48,16},{64,96},{80,112},{96,64},{112,80},{1... | collective-permute-start | bytes 442376 | tf_op jit(solution)/shard_map/ppermute | solution.py:28
  94.5 4.3 %collective-permute-start.6 = (bf16[2,4,6,1536]{3,1,2,0:T(4,128)(2,1)S(1)}, bf16[2,4,6,1536]{3,1,2,0:T(4,128)(2,1)S(1)}, u32[]{:S(2)}, u32[]{:S(2)}) collective-permute-start(bf16[2,4,6,1536]{3,1,2,0:T(4,128)(2,1)S(1)} %get-tuple-element.24), channel_id=1, source_target_pairs={{0,64},{16,80},{32,96},{48,112},{64,0},{80,16},{96,32},{112,48},{1... | collective-permute-start | bytes 442376 | tf_op jit(solution)/shard_map/ppermute | solution.py:28
  99.7 5.6 %collective-permute-start.7 = (bf16[1,8,6,1536]{3,1,2,0:T(8,128)(2,1)S(1)}, bf16[1,8,6,1536]{3,1,2,0:T(8,128)(2,1)S(1)}, u32[]{:S(2)}, u32[]{:S(2)}) collective-permute-start(bf16[1,8,6,1536]{3,1,2,0:T(8,128)(2,1)S(1)} %bitcast.82), channel_id=1, source_target_pairs={{0,128},{16,144},{32,160},{48,176},{64,192},{80,208},{96,224},{112... | collective-permute-start | bytes 442376 | tf_op jit(solution)/shard_map/ppermute | solution.py:28
  111.9 12.8 %all-to-all-start.1 = ((bf16[16,6,1536]{2,1,0:T(8,128)(2,1)}), bf16[16,6,1536]{2,1,0:T(8,128)(2,1)S(1)}, u32[]{:S(2)}, u32[]{:S(2)}) async-start(bf16[16,6,1536]{2,1,0:T(8,128)(2,1)} %reshape.63), calls=%async_computation.1 | async-start | bytes 786432 | tf_op jit(solution)/shard_map/all_to_all | solution.py:19
  167.7 2.3 %copy-start = (bf16[1536,1536]{1,0:T(8,128)(2,1)S(1)}, bf16[1536,1536]{1,0:T(8,128)(2,1)}, u32[]{:S(2)}) copy-start(bf16[1536,1536]{1,0:T(8,128)(2,1)} %all-gather.2.cloned.1.call-done.whole_ref) | copy-start | bytes 14155780
Sparse Core Ops, SparseCore 0:
  111.1 56.5 all-gather.1
